TPU v7x, 512 devices: a whole 4x4x16 slice. The times are simulated.
512 devices in a mesh: enc: 16 (over x, z_hi), seq: 8 (over y, core), tp: 4 (over z_lo).
Axes of the slice: x: 4, y: 4, z: 16 (z_hi: 4, z_lo: 4; z = z_hi * 4 + z_lo), core: 2. Of those that a mesh axis runs over, the one named last changes fastest.
Arguments:
- visual_key_value: bfloat16 [16, 16, 256, 2048], P(None, 'seq', 'enc', 'tp'), may hold values from -4.5 to 4.5
- patch_blocks: int32 [16, 16], P('enc'), may hold values from 1 to 8
- queries: bfloat16 [16, 16, 32, 8192], P('enc', 'seq', None, 'tp'), may hold values from -113 to 113
- suffix_key_value: bfloat16 [16, 16, 32, 2048], P('enc', 'seq', None, 'tp'), may hold values from -6 to 6
- suffix_hidden_state: bfloat16 [16, 16, 32, 8192], P('enc', 'seq', None, 'tp'), may hold values from -6 to 6
- down_weight: bfloat16 [8192, 128], P('tp'), may hold values from -0.0625 to 0.0625
- up_weight: bfloat16 [128, 8192], P(None, 'tp'), may hold values from -1.5 to 1.5
- question_adapter: int32 [16, 16], P('enc', 'seq'), may hold values from 0 to 7
- suffix_token_length: int32 [16, 16], P('enc', 'seq'), may hold values from 1 to 32
Outputs:
- context: bfloat16 [16, 16, 32, 8192], P('enc', 'seq', None, 'tp')
All inputs are finite; a program needn't handle non-finite values.
Results may differ from a plain program's by a relative error of at most 0.0087.
Values may be sent and summed in bfloat16 or wider, within the bound.
A program may use at most 64 MiB of HBM per device.

v0:
```python
import math
import jax
import jax.numpy as jnp
from jax import lax
from jax.sharding import PartitionSpec as P

HEAD_SIZE = 128
ADAPTER_RANK = 16
NEG_BIG = -1e30
ADAPTER_SCALE = 2.0


def sent_to_all(shard, axis):
    copies = jnp.broadcast_to(shard, (lax.axis_size(axis), *shard.shape))
    return lax.all_to_all(copies, axis, split_axis=0, concat_axis=0, tiled=True)


def over_copies(shard, axis):
    return sent_to_all(shard, axis).sum(axis=0)


def per_device(
    visual_key_value,
    patch_blocks,
    queries,
    suffix_key_value,
    suffix_hidden_state,
    down_weight,
    up_weight,
    question_adapter,
    suffix_token_length,
):
    docs_here, asked_here, suffix_len, query_feature_width = queries.shape
    kv_local = suffix_key_value.shape[3] // (2 * HEAD_SIZE)
    head_group = query_feature_width // (kv_local * HEAD_SIZE)
    asked_rows = asked_here * suffix_len
    row_totals = docs_here * asked_rows
    inverse = 1.0 / math.sqrt(HEAD_SIZE)
    enc_count = lax.axis_size("enc")
    hidden_state_rows = suffix_hidden_state.reshape(row_totals, suffix_hidden_state.shape[3])
    reduced_features = jnp.dot(hidden_state_rows, down_weight, preferred_element_type=jnp.float32)
    owning_question = lax.broadcasted_iota(jnp.int32, (1, down_weight.shape[1]), 1) // ADAPTER_RANK
    row_ids = jnp.broadcast_to(
        question_adapter[:, :, None], (docs_here, asked_here, suffix_len)
    ).reshape(row_totals, 1)
    reduced_features = jnp.where(owning_question == row_ids, reduced_features, 0.0)
    selected_adapter = over_copies(reduced_features, "tp").astype(jnp.bfloat16)
    raised_features = jnp.dot(selected_adapter, up_weight, preferred_element_type=jnp.float32)
    query_matrix = (
        queries.reshape(row_totals, query_feature_width).astype(jnp.float32)
        + ADAPTER_SCALE * raised_features
    ).astype(jnp.bfloat16)
    query_matrix = query_matrix.reshape(docs_here, asked_rows, kv_local, head_group, HEAD_SIZE)
    suffix_pairs = suffix_key_value.reshape(
        docs_here, asked_here, suffix_len, kv_local, 2, HEAD_SIZE
    )
    query_split = query_matrix.reshape(
        docs_here, asked_here, suffix_len, kv_local, head_group, HEAD_SIZE
    )
    suffix_scores = (
        jnp.einsum(
            "bqikgd,bqjkd->bkgqij",
            query_split,
            suffix_pairs[:, :, :, :, 0, :],
            preferred_element_type=jnp.float32,
        )
        * inverse
    )
    positions = lax.broadcasted_iota(jnp.int32, (suffix_len, suffix_len), 0)
    columns = lax.broadcasted_iota(jnp.int32, (suffix_len, suffix_len), 1)
    causal = columns <= positions
    within = (
        lax.broadcasted_iota(jnp.int32, (1, 1, suffix_len), 2) < suffix_token_length[:, :, None]
    )
    suffix_mask = (causal[None, None, :, :] & within[:, :, None, :])[:, None, None]
    suffix_scores = jnp.where(suffix_mask, suffix_scores, NEG_BIG)
    suffix_peak = suffix_scores.max(axis=-1)
    suffix_weights = jnp.where(suffix_mask, jnp.exp(suffix_scores - suffix_peak[..., None]), 0.0)
    running = suffix_peak.reshape(docs_here, kv_local, head_group, asked_rows)
    totals = suffix_weights.sum(axis=-1).reshape(docs_here, kv_local, head_group, asked_rows)
    numerators = jnp.einsum(
        "bkgqij,bqjkd->bkgqid",
        suffix_weights.astype(jnp.bfloat16),
        suffix_pairs[:, :, :, :, 1, :],
        preferred_element_type=jnp.float32,
    )
    numerators = numerators.reshape(docs_here, kv_local, head_group, asked_rows, HEAD_SIZE)
    carried = (running, totals, numerators)
    exchanged = lax.all_to_all(visual_key_value, "enc", split_axis=0, concat_axis=0, tiled=True)
    key_piece = lax.all_gather(exchanged, "seq", axis=1, tiled=True)
    peaks_now, totals_now, numer_now = carried
    tile_rows, page_count, tile_len, piece_width = key_piece.shape
    key_values = key_piece.reshape(enc_count, docs_here, page_count, tile_len, piece_width)
    key_values = jnp.moveaxis(key_values, 1, 0).reshape(
        docs_here, enc_count * page_count * tile_len, kv_local, 2, HEAD_SIZE
    )
    token_pos = lax.broadcasted_iota(
        jnp.int32, (1, enc_count, 1, tile_len), 1
    ) * tile_len + lax.broadcasted_iota(jnp.int32, (1, enc_count, 1, tile_len), 3)
    live_keys = 8 * token_pos < patch_blocks[:, None, :, None] * (enc_count * tile_len)
    live_keys = live_keys.reshape(docs_here, 1, 1, 1, enc_count * page_count * tile_len)
    scores = (
        jnp.einsum(
            "bnkgd,blkd->bkgnl",
            query_matrix,
            key_values[:, :, :, 0, :],
            preferred_element_type=jnp.float32,
        )
        * inverse
    )
    scores = jnp.where(live_keys, scores, NEG_BIG)
    updated = jnp.maximum(peaks_now, scores.max(axis=-1))
    rescale = jnp.exp(peaks_now - updated)
    weights = jnp.where(live_keys, jnp.exp(scores - updated[..., None]), 0.0)
    totals_next = totals_now * rescale + weights.sum(axis=-1)
    numer_next = numer_now * rescale[..., None] + jnp.einsum(
        "bkgnl,blkd->bkgnd",
        weights.astype(jnp.bfloat16),
        key_values[:, :, :, 1, :],
        preferred_element_type=jnp.float32,
    )
    carried = (updated, totals_next, numer_next)
    running, totals, numerators = carried
    context = numerators / totals[..., None]
    context = jnp.transpose(context, (0, 3, 1, 2, 4)).reshape(
        docs_here, asked_here, suffix_len, query_feature_width
    )
    kept_rows = (
        lax.broadcasted_iota(jnp.int32, (1, 1, suffix_len), 2) < suffix_token_length[:, :, None]
    )
    return jnp.where(kept_rows[:, :, :, None], context, 0.0).astype(jnp.bfloat16)


def solution(mesh):
    placed = (
        P(None, "seq", "enc", "tp"),
        P("enc", None),
        P("enc", "seq", None, "tp"),
        P("enc", "seq", None, "tp"),
        P("enc", "seq", None, "tp"),
        P("tp", None),
        P(None, "tp"),
        P("enc", "seq"),
        P("enc", "seq"),
    )
    return jax.shard_map(
        per_device,
        mesh=mesh,
        in_specs=placed,
        out_specs=P("enc", "seq", None, "tp"),
        check_vma=False,
    )
```

profile of v0, /device:TPU:1, one launch (start us, length us, event | category | flops | bytes accessed | tf_op | source)
XLA Modules:
  0.0 128.2 jit_solution(13732557373285925791)
XLA Ops:
  6.5 0.0 copy-start
  6.5 0.0 all-gather.2.cloned.1.call-start
  6.5 45.5 %all_to_all.10 = bf16[16,2,16,512]{3,2,1,0:T(8,128)(2,1)} all-to-all(bf16[16,2,16,512]{3,2,1,0:T(8,128)(2,1)} %param.9), channel_id=1, replica_groups=mesh['enc'=16,'seq'=8,'tp'=4] {'enc'}, dimensions={0} | all-to-all | bytes 1048576 | tf_op jit(solution)/shard_map/all_to_all | solution.py:89
  52.1 0.0 all-gather.2.cloned.1.call-update
  52.1 0.7 broadcast_in_dim.81
  52.8 0.1 broadcast_in_dim.82
  52.9 1.3 %convolution_select_fusion = f32[64,128]{1,0:T(8,128)S(1)} fusion(bf16[64,2048]{1,0:T(8,128)(2,1)} %bitcast.147, bf16[2048,128]{1,0:T(8,128)(2,1)} %param.14, s32[128]{0:T(128)S(1)} %and_select_fusion, s32[64]{0:T(128)S(1)} %broadcast_in_dim.82), kind=kOutput, calls=%fused_computation.24 | convolution fusion | flops 33570816 | bytes 819968 | tf_op jit(solution)/shard_map/dot_general | solution.py:41
  54.3 0.7 broadcast_in_dim.84
  54.9 9.1 %all-to-all-start = ((f32[4,64,128]{2,1,0:T(8,128)}), f32[4,64,128]{2,1,0:T(8,128)S(1)}, u32[]{:S(2)}, u32[]{:S(2)}) async-start(f32[4,64,128]{2,1,0:T(8,128)} %broadcast_in_dim.84), calls=%async_computation | async-start | bytes 262144 | tf_op jit(solution)/shard_map/all_to_all | solution.py:15
  64.0 0.7 multiply_bitcast_fusion
  64.7 0.1 add_multiply_fusion
  64.8 0.1 broadcast_compare_fusion
  64.9 0.1 lt.61
  65.0 0.9 reshape.308
  65.9 0.7 iota_compare_fusion.1
  66.6 0.1 fusion.39
  66.7 2.1 %all-to-all-done = f32[4,64,128]{2,1,0:T(8,128)S(1)} async-done(((f32[4,64,128]{2,1,0:T(8,128)}), f32[4,64,128]{2,1,0:T(8,128)S(1)}, u32[]{:S(2)}, u32[]{:S(2)}) %all-to-all-start) | async-done | bytes 131104 | tf_op jit(solution)/shard_map/all_to_all | solution.py:15
  68.8 0.0 copy-done
  68.8 1.2 fusion.17
  70.1 0.4 fusion.40
  70.4 0.4 fusion.25
  70.8 0.2 convolution_bitcast_fusion
  71.1 19.3 %all-gather.2.cloned.1.call-done = bf16[16,16,16,512]{3,2,1,0:T(8,128)(2,1)} async-done(((bf16[16,2,16,512]{3,2,1,0:T(8,128)(2,1)}), bf16[16,16,16,512]{3,2,1,0:T(8,128)(2,1)}) %all-gather.2.cloned.1.call-update) | async-done | bytes 4194320 | tf_op jit(solution)/shard_map/all_gather | solution.py:90
  90.3 6.9 %reshape_transpose_reshape.3 = bf16[1,4096,2,2,128]{4,3,2,1,0:T(2,128)(2,1)} reshape(bf16[16,16,16,512]{3,2,1,0:T(8,128)(2,1)} %all-gather.2.cloned.1.call-done) | data formatting | bytes 8388608 | tf_op jit(solution)/shard_map/reshape;transpose;reshape | solution.py:94
  97.2 9.0 %fusion.38 = (bf16[1,4096,2,1,128]{4,3,2,1,0:T(2,128)(2,1)S(1)}, bf16[1,4096,2,1,128]{4,3,2,1,0:T(2,128)(2,1)S(1)}) fusion(bf16[1,4096,2,2,128]{4,3,2,1,0:T(2,128)(2,1)} %reshape_transpose_reshape.3), kind=kLoop, calls=%fused_computation.56 | loop fusion | bytes 8388608 | tf_op jit(solution)/shard_map/slice | solution.py:106
  106.2 2.9 %fusion.1 = (f32[2,8,64]{1,2,0:T(8,128)S(1)}, f32[2,64,8,4096]{3,2,1,0:T(8,128)S(1)}) fusion(pred[4096]{0:T(1024)(128)(4,1)S(1)} %lt.61, bf16[1,4096,2,1,128]{4,3,2,1,0:T(2,128)(2,1)S(1)} %get-tuple-element.7, bf16[64,2,8,128]{3,2,1,0:T(8,128)(2,1)S(1)} %bitcast.143), kind=kOutput, calls=%fused_computation.3 | convolution fusion | flops 1086323712 | bytes 19144704 | tf_op jit(solution)/shard_map/bnkgd,blkd->bkgnl/dot_general | solution.py:103
  109.2 4.9 %fusion.2 = f32[2,8,64]{1,2,0:T(8,128)S(1)} fusion(f32[2,64,8,4096]{3,2,1,0:T(8,128)S(1)} %get-tuple-element.16, f32[2,8,64]{1,2,0:T(8,128)S(1)} %max.17, pred[4096]{0:T(1024)(128)(4,1)S(1)} %lt.61), kind=kLoop, calls=%fused_computation.4 | loop fusion | flops 20970496 | bytes 16789504 | tf_op jit(solution)/shard_map/reduce_sum | solution.py:115
  114.1 4.8 %fusion.21 = f32[1,64,2,8,128]{4,3,1,2,0:T(8,128)} fusion(bf16[1,4096,2,1,128]{4,3,2,1,0:T(2,128)(2,1)S(1)} %get-tuple-element.8, f32[2,64,8,4096]{3,2,1,0:T(8,128)S(1)} %get-tuple-element.16, f32[2,8,64]{1,2,0:T(8,128)S(1)} %max.17, pred[4096]{0:T(1024)(128)(4,1)S(1)} %lt.61, f32[2,8,64,128]{3,2,1,0:T(8,128)S(1)} %bitcast.146, ...), kind=kOutput, calls=%fused_computation.23 | convolution fusion | flops 1095106560 | bytes 19939328 | tf_op jit(solution)/shard_map/bkgnl,blkd->bkgnd/dot_general | solution.py:116
  118.9 1.1 copy.38
  120.0 0.5 fusion.24
  120.5 0.9 copy.39
  (9 shorter events, 0.1 us)
Async XLA Ops:
  6.5 62.3 %copy-start = (bf16[128,2048]{1,0:T(8,128)(2,1)S(1)}, bf16[128,2048]{1,0:T(8,128)(2,1)}, u32[]{:S(2)}) copy-start(bf16[128,2048]{1,0:T(8,128)(2,1)} %param.15) | copy-start | bytes 1572868
  6.5 83.8 %all-gather.2.cloned.1.call-start = ((), (), s32[]{:S(2)}) async-start(), calls=%async_computation.2 | async-start | bytes 4718592 | tf_op jit(solution)/shard_map/all_gather | solution.py:90
  54.9 13.9 %all-to-all-start = ((f32[4,64,128]{2,1,0:T(8,128)}), f32[4,64,128]{2,1,0:T(8,128)S(1)}, u32[]{:S(2)}, u32[]{:S(2)}) async-start(f32[4,64,128]{2,1,0:T(8,128)} %broadcast_in_dim.84), calls=%async_computation | async-start | bytes 262144 | tf_op jit(solution)/shard_map/all_to_all | solution.py:15
Sparse Core Ops, SparseCore 0:
  52.2 38.0 all-gather.1
where the time goes:
time: 129 us; the launch traced here: 128 us
  blocking collectives  45.5 us (35%)
  waiting for transfers between devices  21.4 us (17%)
  local copies, waits for them, and re-layouts  20.4 us (16%)
  between operations  13.5 us (10%)
  matrix products  10.8 us (8%)
  starting transfers between devices  9.1 us (7%)
  other arithmetic  7.44 us (6%)
    all_to_all x1, blocking collectives, per_device(): lax.all_to_all(visual_key_value, 'enc', split_axis=0, concat_axis=0, tile...  45.5 us
    all_gather x1, waiting for transfers between devices, per_device(): key_piece = lax.all_gather(exchanged, 'seq', axis=1, tiled=True)  19.3 us
    all_to_all x1, starting transfers between devices, sent_to_all(): return lax.all_to_all(copies, axis, split_axis=0, concat_axis=0, tiled=True)  9.1 us
    slice x1, local copies, waits for them, and re-layouts, per_device(): key_values[:, :, :, 0, :]  8.97 us
    another operation x1, local copies, waits for them, and re-layouts, per_device(): jnp.moveaxis(key_values, 1, 0)  6.92 us
    reduce_sum x1, other arithmetic, per_device(): totals_next = totals_now * rescale + weights.sum(axis=-1)  4.91 us
    dot_general x1, matrix products, per_device(): jnp.einsum('bkgnl,blkd->bkgnd', weights.astype(jnp.bfloat16), key_values[...  4.77 us
    dot_general x1, matrix products, per_device(): jnp.einsum('bnkgd,blkd->bkgnl', query_matrix, key_values[:, :, :, 0, :],...  2.92 us
  transfers between devices with their start and end apart: 2, of which 2 were waited for; matrix products, arithmetic and copies ran while one was open for 6% of the time, Pallas kernels for 0%

commit v1 on v0

--- a/solution.py
+++ b/solution.py
@@ -87,7 +87,12 @@
     numerators = numerators.reshape(docs_here, kv_local, head_group, asked_rows, HEAD_SIZE)
     carried = (running, totals, numerators)
     exchanged = lax.all_to_all(visual_key_value, "enc", split_axis=0, concat_axis=0, tiled=True)
-    key_piece = lax.all_gather(exchanged, "seq", axis=1, tiled=True)
+    ring = [exchanged]
+    for hop in range(7):
+        ring.append(lax.ppermute(ring[-1], "seq", [(dev, (dev + 1) % 8) for dev in range(8)]))
+    key_piece = jnp.roll(
+        jnp.concatenate(ring[::-1], axis=1), (lax.axis_index("seq") + 1) * ring[0].shape[1], axis=1
+    )
     peaks_now, totals_now, numer_now = carried
     tile_rows, page_count, tile_len, piece_width = key_piece.shape
     key_values = key_piece.reshape(enc_count, docs_here, page_count, tile_len, piece_width)

time: 129 us -> 162 us (1.26)
  the two profiles are of different devices: /device:TPU:1 before, /device:TPU:32 now
where the time goes in v1:
time: 162 us; the launch traced here: 161 us
  waiting for transfers between devices  55.3 us (34%)
  blocking collectives  51 us (31%)
  local copies, waits for them, and re-layouts  31.7 us (20%)
  matrix products  12 us (7%)
  other arithmetic  7.41 us (5%)
  starting transfers between devices  3.74 us (2%)
    ppermute x7, waiting for transfers between devices, per_device(): lax.ppermute(ring[-1], 'seq', [(dev, (dev + 1) % 8) for dev in range(8)])  55.3 us
    all_to_all x1, blocking collectives, per_device(): lax.all_to_all(visual_key_value, 'enc', split_axis=0, concat_axis=0, tile...  51 us
    slice x1, local copies, waits for them, and re-layouts, per_device(): key_values[:, :, :, 0, :]  8.9 us
    unnamed x24, local copies, waits for them, and re-layouts  8.65 us
    another operation x1, local copies, waits for them, and re-layouts, per_device(): jnp.moveaxis(key_values, 1, 0)  6.94 us
    reduce_sum x1, other arithmetic, per_device(): totals_next = totals_now * rescale + weights.sum(axis=-1)  4.9 us
    dot_general x1, matrix products, per_device(): jnp.einsum('bnkgd,blkd->bkgnl', query_matrix, key_values[:, :, :, 0, :],...  4.11 us
    dot_general x1, matrix products, per_device(): jnp.einsum('bkgnl,blkd->bkgnd', weights.astype(jnp.bfloat16), key_values[...  3.81 us
  transfers between devices with their start and end apart: 8, of which 7 were waited for; matrix products, arithmetic and copies ran while one was open for 6% of the time, Pallas kernels for 0%

profile of v1, /device:TPU:32, one launch (start us, length us, event | category | flops | bytes accessed | tf_op | source)
XLA Modules:
  0.0 161.4 jit_solution(14178566122234080584)
XLA Ops:
  0.0 0.0 copy-start
  0.0 51.0 %all_to_all.10 = bf16[16,2,16,512]{3,2,1,0:T(8,128)(2,1)S(1)} all-to-all(bf16[16,2,16,512]{3,2,1,0:T(8,128)(2,1)} %param.9), channel_id=1, replica_groups=mesh['enc'=16,'seq'=8,'tp'=4] {'enc'}, dimensions={0} | all-to-all | bytes 1048576 | tf_op jit(solution)/shard_map/all_to_all | solution.py:89
  51.0 0.0 collective-permute-start
  51.0 9.8 %collective-permute-done = bf16[16,2,16,512]{3,2,1,0:T(8,128)(2,1)S(1)} collective-permute-done((bf16[16,2,16,512]{3,2,1,0:T(8,128)(2,1)S(1)}, bf16[16,2,16,512]{3,2,1,0:T(8,128)(2,1)S(1)}, u32[]{:S(2)}, u32[]{:S(2)}) %collective-permute-start) | collective-permute-done | bytes 524320 | tf_op jit(solution)/shard_map/ppermute | solution.py:92
  60.8 0.0 collective-permute-start.1
  60.8 9.8 %collective-permute-done.1 = bf16[16,2,16,512]{3,2,1,0:T(8,128)(2,1)S(1)} collective-permute-done((bf16[16,2,16,512]{3,2,1,0:T(8,128)(2,1)S(1)}, bf16[16,2,16,512]{3,2,1,0:T(8,128)(2,1)S(1)}, u32[]{:S(2)}, u32[]{:S(2)}) %collective-permute-start.1) | collective-permute-done | bytes 524320 | tf_op jit(solution)/shard_map/ppermute | solution.py:92
  70.7 0.0 collective-permute-start.2
  70.7 0.7 broadcast_in_dim.81
  71.4 0.1 broadcast_in_dim.82
  71.5 1.3 convolution_select_fusion
  72.8 0.7 broadcast_in_dim.84
  73.5 3.7 %all-to-all-start = ((f32[4,64,128]{2,1,0:T(8,128)}), f32[4,64,128]{2,1,0:T(8,128)S(1)}, u32[]{:S(2)}, u32[]{:S(2)}) async-start(f32[4,64,128]{2,1,0:T(8,128)} %broadcast_in_dim.84), calls=%async_computation | async-start | bytes 262144 | tf_op jit(solution)/shard_map/all_to_all | solution.py:15
  77.2 3.3 %collective-permute-done.2 = bf16[16,2,16,512]{3,2,1,0:T(8,128)(2,1)S(1)} collective-permute-done((bf16[16,2,16,512]{3,2,1,0:T(8,128)(2,1)S(1)}, bf16[16,2,16,512]{3,2,1,0:T(8,128)(2,1)S(1)}, u32[]{:S(2)}, u32[]{:S(2)}) %collective-permute-start.2) | collective-permute-done | bytes 524320 | tf_op jit(solution)/shard_map/ppermute | solution.py:92
  80.5 0.0 collective-permute-start.3
  80.5 0.7 multiply_bitcast_fusion
  81.1 0.1 add_multiply_fusion
  81.2 9.1 %collective-permute-done.3 = bf16[16,2,16,512]{3,2,1,0:T(8,128)(2,1)S(1)} collective-permute-done((bf16[16,2,16,512]{3,2,1,0:T(8,128)(2,1)S(1)}, bf16[16,2,16,512]{3,2,1,0:T(8,128)(2,1)S(1)}, u32[]{:S(2)}, u32[]{:S(2)}) %collective-permute-start.3) | collective-permute-done | bytes 524320 | tf_op jit(solution)/shard_map/ppermute | solution.py:92
  90.3 0.0 copy-start.1
  90.3 0.0 collective-permute-start.4
  90.3 0.1 broadcast_compare_fusion
  90.4 0.1 lt.73
  90.5 0.9 reshape.308
  91.4 0.7 iota_compare_fusion.1
  92.1 8.1 %collective-permute-done.4 = bf16[16,2,16,512]{3,2,1,0:T(8,128)(2,1)} collective-permute-done((bf16[16,2,16,512]{3,2,1,0:T(8,128)(2,1)S(1)}, bf16[16,2,16,512]{3,2,1,0:T(8,128)(2,1)}, u32[]{:S(2)}, u32[]{:S(2)}) %collective-permute-start.4) | collective-permute-done | bytes 524320 | tf_op jit(solution)/shard_map/ppermute | solution.py:92
  100.2 0.0 collective-permute-start.5
  100.2 0.1 fusion.36
  100.3 0.0 all-to-all-done
  100.4 0.0 copy-done
  100.4 1.2 fusion.17
  101.6 0.7 copy.61
  102.3 8.0 %collective-permute-done.5 = bf16[16,2,16,512]{3,2,1,0:T(8,128)(2,1)} collective-permute-done((bf16[16,2,16,512]{3,2,1,0:T(8,128)(2,1)}, bf16[16,2,16,512]{3,2,1,0:T(8,128)(2,1)}, u32[]{:S(2)}, u32[]{:S(2)}) %collective-permute-start.5) | collective-permute-done | bytes 524320 | tf_op jit(solution)/shard_map/ppermute | solution.py:92
  110.3 0.0 collective-permute-start.6
  110.3 0.0 copy-done.1
  110.4 1.3 fusion.37
  111.7 0.1 copy.48
  111.7 0.4 fusion.25
  112.1 0.0 copy-start.2
  112.1 0.2 convolution_bitcast_fusion
  112.4 0.9 copy.44
  113.2 0.1 copy.50
  113.3 7.2 %collective-permute-done.6 = bf16[16,2,16,512]{3,2,1,0:T(8,128)(2,1)} collective-permute-done((bf16[16,2,16,512]{3,2,1,0:T(8,128)(2,1)}, bf16[16,2,16,512]{3,2,1,0:T(8,128)(2,1)}, u32[]{:S(2)}, u32[]{:S(2)}) %collective-permute-start.6) | collective-permute-done | bytes 524320 | tf_op jit(solution)/shard_map/ppermute | solution.py:92
  120.5 1.1 constant_dynamic-update-slice_fusion.15
  121.6 1.1 constant_dynamic-update-slice_fusion.14
  122.7 1.1 constant_dynamic-update-slice_fusion.13
  123.7 1.1 constant_dynamic-update-slice_fusion.12
  125.0 1.1 constant_dynamic-update-slice_fusion.7
  126.1 1.1 constant_dynamic-update-slice_fusion.6
  127.2 1.1 constant_dynamic-update-slice_fusion.5
  128.3 0.0 copy-done.2
  128.5 2.4 %constant_dynamic-slice_fusion = bf16[16,16,16,512]{3,2,1,0:T(8,128)(2,1)} fusion(bf16[16,32,16,512]{3,2,1,0:T(8,128)(2,1)S(1)} %constant_dynamic-update-slice_fusion, s32[]{:T(128)S(6)} %select_n.61), kind=kLoop, calls=%fused_computation.67 | loop fusion | bytes 8388612 | tf_op jit(solution)/shard_map/jit(_roll_dynamic)/dynamic_slice | solution.py:93
  131.0 6.9 %reshape_transpose_reshape.3 = bf16[1,4096,2,2,128]{4,3,2,1,0:T(2,128)(2,1)} reshape(bf16[16,16,16,512]{3,2,1,0:T(8,128)(2,1)} %constant_dynamic-slice_fusion) | data formatting | bytes 8388608 | tf_op jit(solution)/shard_map/reshape;transpose;reshape | solution.py:99
  137.9 8.9 %fusion.35 = (bf16[1,4096,2,1,128]{4,3,2,1,0:T(2,128)(2,1)S(1)}, bf16[1,4096,2,1,128]{4,3,2,1,0:T(2,128)(2,1)S(1)}) fusion(bf16[1,4096,2,2,128]{4,3,2,1,0:T(2,128)(2,1)} %reshape_transpose_reshape.3), kind=kLoop, calls=%fused_computation.71 | loop fusion | bytes 8388608 | tf_op jit(solution)/shard_map/slice | solution.py:111
  146.8 4.1 %bitcast_reduce_fusion = (f32[2,8,64]{2,1,0:T(8,128)S(1)}, f32[2,4096,64,8]{1,2,3,0:T(8,128)S(1)}) fusion(pred[4096]{0:T(1024)(128)(4,1)S(1)} %lt.73, bf16[64,2,8,128]{3,2,1,0:T(8,128)(2,1)} %bitcast.54, bf16[1,4096,2,1,128]{4,3,2,1,0:T(2,128)(2,1)S(1)} %get-tuple-element.7), kind=kOutput, calls=%fused_computation.1 | convolution fusion | flops 1086323712 | bytes 19144704 | tf_op jit(solution)/shard_map/bnkgd,blkd->bkgnl/dot_general | solution.py:108
  150.9 0.0 copy-start.3
  151.0 4.9 %fusion.2 = f32[2,8,64]{2,1,0:T(8,128)S(1)} fusion(f32[2,4096,64,8]{1,2,3,0:T(8,128)S(1)} %get-tuple-element.16, f32[2,8,64]{2,1,0:T(8,128)S(1)} %max.17, pred[4096]{0:T(1024)(128)(4,1)S(1)} %lt.73), kind=kLoop, calls=%fused_computation.5 | loop fusion | flops 20970496 | bytes 16789504 | tf_op jit(solution)/shard_map/reduce_sum | solution.py:120
  155.9 0.0 copy-done.3
  155.9 3.8 %fusion.21 = f32[1,64,2,8,128]{4,1,3,2,0:T(8,128)S(1)} fusion(bf16[1,4096,2,1,128]{4,3,2,1,0:T(2,128)(2,1)S(1)} %get-tuple-element.8, f32[2,4096,64,8]{1,2,3,0:T(8,128)S(1)} %get-tuple-element.16, f32[2,8,64]{2,1,0:T(8,128)S(1)} %max.17, pred[4096]{0:T(1024)(128)(4,1)S(1)} %lt.73, f32[2,8,64,128]{3,2,1,0:T(8,128)S(1)} %bitcast.134, ...), kind=kOutput, calls=%fused_computation.24 | convolution fusion | flops 1095106560 | bytes 19939328 | tf_op jit(solution)/shard_map/bkgnl,blkd->bkgnd/dot_general | solution.py:121
  159.7 0.3 copy.51
  160.0 0.5 fusion.24
  160.5 0.9 copy.52
  (16 shorter events, 0.4 us)
Async XLA Ops:
  0.0 100.4 %copy-start = (bf16[128,2048]{1,0:T(8,128)(2,1)S(1)}, bf16[128,2048]{1,0:T(8,128)(2,1)}, u32[]{:S(2)}) copy-start(bf16[128,2048]{1,0:T(8,128)(2,1)} %param.15) | copy-start | bytes 1572868
  51.0 9.8 %collective-permute-start = (bf16[16,2,16,512]{3,2,1,0:T(8,128)(2,1)S(1)}, bf16[16,2,16,512]{3,2,1,0:T(8,128)(2,1)S(1)}, u32[]{:S(2)}, u32[]{:S(2)}) collective-permute-start(bf16[16,2,16,512]{3,2,1,0:T(8,128)(2,1)S(1)} %all_to_all.10), channel_id=1, source_target_pairs={{0,4},{4,8},{8,12},{12,16},{16,20},{20,24},{24,28},{28,0},{1,5},{5... | collective-permute-start | bytes 1572872 | tf_op jit(solution)/shard_map/ppermute | solution.py:92
  60.8 9.8 %collective-permute-start.1 = (bf16[16,2,16,512]{3,2,1,0:T(8,128)(2,1)S(1)}, bf16[16,2,16,512]{3,2,1,0:T(8,128)(2,1)S(1)}, u32[]{:S(2)}, u32[]{:S(2)}) collective-permute-start(bf16[16,2,16,512]{3,2,1,0:T(8,128)(2,1)S(1)} %collective-permute-done), channel_id=1, source_target_pairs={{0,4},{4,8},{8,12},{12,16},{16,20},{20,24},{24,28},{28,0},{1,5},{5... | collective-permute-start | bytes 1572872 | tf_op jit(solution)/shard_map/ppermute | solution.py:92
  70.7 9.8 %collective-permute-start.2 = (bf16[16,2,16,512]{3,2,1,0:T(8,128)(2,1)S(1)}, bf16[16,2,16,512]{3,2,1,0:T(8,128)(2,1)S(1)}, u32[]{:S(2)}, u32[]{:S(2)}) collective-permute-start(bf16[16,2,16,512]{3,2,1,0:T(8,128)(2,1)S(1)} %collective-permute-done.1), channel_id=1, source_target_pairs={{0,4},{4,8},{8,12},{12,16},{16,20},{20,24},{24,28},{28,0},{1,5},{5... | collective-permute-start | bytes 1572872 | tf_op jit(solution)/shard_map/ppermute | solution.py:92
  73.5 26.8 %all-to-all-start = ((f32[4,64,128]{2,1,0:T(8,128)}), f32[4,64,128]{2,1,0:T(8,128)S(1)}, u32[]{:S(2)}, u32[]{:S(2)}) async-start(f32[4,64,128]{2,1,0:T(8,128)} %broadcast_in_dim.84), calls=%async_computation | async-start | bytes 262144 | tf_op jit(solution)/shard_map/all_to_all | solution.py:15
  80.5 9.8 %collective-permute-start.3 = (bf16[16,2,16,512]{3,2,1,0:T(8,128)(2,1)S(1)}, bf16[16,2,16,512]{3,2,1,0:T(8,128)(2,1)S(1)}, u32[]{:S(2)}, u32[]{:S(2)}) collective-permute-start(bf16[16,2,16,512]{3,2,1,0:T(8,128)(2,1)S(1)} %collective-permute-done.2), channel_id=1, source_target_pairs={{0,4},{4,8},{8,12},{12,16},{16,20},{20,24},{24,28},{28,0},{1,5},{5... | collective-permute-start | bytes 1572872 | tf_op jit(solution)/shard_map/ppermute | solution.py:92
  90.3 20.1 %copy-start.1 = (bf16[16,2,16,512]{3,2,1,0:T(8,128)(2,1)}, bf16[16,2,16,512]{3,2,1,0:T(8,128)(2,1)S(1)}, u32[]{:S(2)}) copy-start(bf16[16,2,16,512]{3,2,1,0:T(8,128)(2,1)S(1)} %collective-permute-done.3) | copy-start | bytes 1572868
  90.3 9.9 %collective-permute-start.4 = (bf16[16,2,16,512]{3,2,1,0:T(8,128)(2,1)S(1)}, bf16[16,2,16,512]{3,2,1,0:T(8,128)(2,1)}, u32[]{:S(2)}, u32[]{:S(2)}) collective-permute-start(bf16[16,2,16,512]{3,2,1,0:T(8,128)(2,1)S(1)} %collective-permute-done.3), channel_id=1, source_target_pairs={{0,4},{4,8},{8,12},{12,16},{16,20},{20,24},{24,28},{28,0},{1,5},{5... | collective-permute-start | bytes 1572872 | tf_op jit(solution)/shard_map/ppermute | solution.py:92
  100.2 10.1 %collective-permute-start.5 = (bf16[16,2,16,512]{3,2,1,0:T(8,128)(2,1)}, bf16[16,2,16,512]{3,2,1,0:T(8,128)(2,1)}, u32[]{:S(2)}, u32[]{:S(2)}) collective-permute-start(bf16[16,2,16,512]{3,2,1,0:T(8,128)(2,1)} %collective-permute-done.4), channel_id=1, source_target_pairs={{0,4},{4,8},{8,12},{12,16},{16,20},{20,24},{24,28},{28,0},{1,5},{5... | collective-permute-start | bytes 1572872 | tf_op jit(solution)/shard_map/ppermute | solution.py:92
  110.3 10.1 %collective-permute-start.6 = (bf16[16,2,16,512]{3,2,1,0:T(8,128)(2,1)}, bf16[16,2,16,512]{3,2,1,0:T(8,128)(2,1)}, u32[]{:S(2)}, u32[]{:S(2)}) collective-permute-start(bf16[16,2,16,512]{3,2,1,0:T(8,128)(2,1)} %collective-permute-done.5), channel_id=1, source_target_pairs={{0,4},{4,8},{8,12},{12,16},{16,20},{20,24},{24,28},{28,0},{1,5},{5... | collective-permute-start | bytes 1572872 | tf_op jit(solution)/shard_map/ppermute | solution.py:92
  112.1 16.2 %copy-start.2 = (bf16[16,2,16,512]{3,2,1,0:T(8,128)(2,1)S(1)}, bf16[16,2,16,512]{3,2,1,0:T(8,128)(2,1)}, u32[]{:S(2)}) copy-start(bf16[16,2,16,512]{3,2,1,0:T(8,128)(2,1)} %copy-done.1) | copy-start | bytes 1572868
  150.9 4.9 %copy-start.3 = (f32[1,2,8,2,32,128]{5,4,3,2,1,0:T(8,128)S(1)}, f32[1,2,8,2,32,128]{5,4,3,2,1,0:T(8,128)}, u32[]{:S(2)}) copy-start(f32[1,2,8,2,32,128]{5,4,3,2,1,0:T(8,128)} %copy.44) | copy-start | bytes 1572868
